TPU v7x, 32 devices: a whole 2x2x4 slice. The times are simulated.
32 devices in a mesh: rows: 8 (over z, y), cols: 4 (over x, core).
Axes of the slice: x: 2, y: 2, z: 4, core: 2. Of those that a mesh axis runs over, the one named last changes fastest.
Arguments:
- matrix: float32 [8192, 10, 512], P('rows', None, 'cols'), may hold values from -6 to 6
Outputs:
- reduced: float32 [8192, 10, 512], P('rows', None, 'cols')
- top_rows: float32 [256, 10, 512], P(None, None, 'cols')
All inputs are finite; a program needn't handle non-finite values.
Results may differ from a plain program's by a relative error of at most 0.0001.
Values sent between devices are 32-bit elements; how exact they have to be, the bound alone decides.
A program may use at most 64 MiB of HBM per device.

v0:
```python
import jax
import jax.numpy as jnp
from jax import lax
from jax.sharding import PartitionSpec as P

PRECISE = lax.Precision.HIGHEST


def spread(block, axis, owner):
    block = jnp.where(lax.axis_index(axis) == owner, block, jnp.zeros_like(block))
    return lax.psum(block, axis)


def product(left, right):
    return jnp.dot(left, right, precision=PRECISE, preferred_element_type=jnp.float32)


def relay_panel(panel_block, root_index):
    return spread(panel_block, "cols", root_index)


def factor(panel, columns):
    gram_block = product(panel.T, panel)
    cross_terms = product(panel.T, columns)
    gram_block, cross_terms = lax.psum((gram_block, cross_terms), "rows")
    triangle = jnp.linalg.cholesky(gram_block)
    weights = jax.scipy.linalg.solve_triangular(triangle, cross_terms, lower=True)
    coefficients = jax.scipy.linalg.solve_triangular(triangle, weights, trans=1, lower=True)
    return (weights, columns - product(panel, coefficients))


def shards(matrix):
    rows_dev, rounds, width = matrix.shape
    columns = matrix.reshape(rows_dev, rounds * width)
    first_panel = relay_panel(columns[:, :width], 0)
    first_rows, columns = factor(first_panel, columns)
    second_panel = relay_panel(columns[:, :width], 1)
    second_rows, columns = factor(second_panel, columns)
    triangle_rows = jnp.concatenate([first_rows, second_rows], axis=0)
    return (
        columns.reshape(rows_dev, rounds, width),
        triangle_rows.reshape(2 * width, rounds, width),
    )


def solution(mesh):
    placed = (P("rows", None, "cols"),)
    return jax.shard_map(
        shards,
        mesh=mesh,
        in_specs=placed,
        out_specs=(P("rows", None, "cols"), P(None, None, "cols")),
        check_vma=False,
    )
```

profile of v0, /device:TPU:2, one launch (start us, length us, event | category | flops | bytes accessed | tf_op | source)
XLA Modules:
  0.0 350.2 jit_solution(4739036694472502393)
XLA Ops:
  7.2 5.9 %copy.10 = f32[1024,10,128]{0,2,1:T(8,128)} copy(f32[1024,10,128]{2,0,1:T(8,128)} %param.6) | data formatting | bytes 10485760 | tf_op args[0]
  13.1 5.9 %copy.14 = f32[1024,1280]{1,0:T(8,128)} copy(f32[1024,1280]{0,1:T(8,128)} %bitcast.45) | data formatting | bytes 10485760 | tf_op jit(solution)/shard_map/reshape | solution.py:34
  19.0 1.9 slice_select_fusion.1
  21.0 33.2 %all-reduce.7.cloned.1.call-done = f32[1024,128]{1,0:T(8,128)} async-done(((f32[1024,128]{1,0:T(8,128)}), f32[1024,128]{1,0:T(8,128)}) %all-reduce.7.cloned.1.call-update) | async-done | bytes 524304 | tf_op jit(solution)/shard_map/psum | solution.py:11
  54.2 8.0 %fusion.13 = f32[128,1280]{1,0:T(8,128)} fusion(f32[1024,128]{1,0:T(8,128)} %all-reduce.7.cloned.1.call-done, f32[1024,1280]{0,1:T(8,128)} %bitcast.46), kind=kOutput, calls=%fused_computation.28 | convolution fusion | flops 2013265920 | bytes 6422528 | tf_op jit(solution)/shard_map/dot_general | solution.py:15
  62.1 1.6 fusion.12
  64.0 75.5 %all-reduce.13.cloned.1.call-done = (f32[128,1280]{1,0:T(8,128)}, f32[128,128]{0,1:T(8,128)}) async-done(((f32[128,1280]{1,0:T(8,128)}, f32[128,128]{0,1:T(8,128)}), (f32[128,1280]{1,0:T(8,128)}, f32[128,128]{0,1:T(8,128)})) %all-reduce.13.cloned.1.call-update) | async-done | bytes 720912 | tf_op jit(solution)/shard_map/psum | solution.py:25
  139.6 0.9 copy.13
  140.5 0.9 fusion.11
  141.4 11.7 %cholesky.44 = f32[128,128]{1,0:T(8,128)S(1)} custom-call(f32[128,128]{1,0:T(8,128)S(1)} %fusion.11), custom_call_target="Cholesky" | custom-call | tf_op jit(solution)/shard_map/jit(cholesky)/cholesky | solution.py:26
  153.7 0.7 fusion
  154.4 9.8 %custom-call.11 = f32[1,128,128]{1,2,0:T(8,128)S(1)} custom-call(f32[1,128,128]{2,1,0:T(8,128)S(1)} %fusion), custom_call_target="InvertDiagBlocksLowerTriangular" | custom-call | tf_op jit(solution)/shard_map/jit(_solve_triangular)/triangular_solve | solution.py:28
  164.2 1.8 fusion.7
  166.0 0.7 fusion.9
  166.7 6.4 %convolution_subtract_fusion.1 = f32[1024,1280]{1,0:T(8,128)S(1)} fusion(f32[1024,1280]{1,0:T(8,128)} %copy.14, f32[1024,128]{1,0:T(8,128)S(1)} %copy-done.1, f32[128,1280]{1,0:T(8,128)S(1)} %fusion.9), kind=kOutput, calls=%fused_computation.1 | convolution fusion | flops 2014576640 | bytes 11665408 | tf_op jit(solution)/shard_map/dot_general | solution.py:15
  173.1 2.3 copy-done
  175.5 0.8 slice_select_fusion
  176.6 30.8 %all-reduce.9.cloned.1.call-done = f32[1024,128]{1,0:T(8,128)} async-done(((f32[1024,128]{1,0:T(8,128)}), f32[1024,128]{1,0:T(8,128)}) %all-reduce.9.cloned.1.call-update) | async-done | bytes 524304 | tf_op jit(solution)/shard_map/psum | solution.py:11
  207.4 2.9 fusion.14
  210.3 6.3 %fusion.15 = f32[128,1280]{1,0:T(8,128)} fusion(f32[1024,128]{1,0:T(8,128)} %all-reduce.9.cloned.1.call-done, f32[1024,1280]{1,0:T(8,128)} %copy-done), kind=kOutput, calls=%fused_computation.30 | convolution fusion | flops 2013265920 | bytes 6422528 | tf_op jit(solution)/shard_map/dot_general | solution.py:15
  216.7 75.8 %all-reduce.11.cloned.1.call-done = (f32[128,1280]{1,0:T(8,128)}, f32[128,128]{0,1:T(8,128)}) async-done(((f32[128,1280]{1,0:T(8,128)}, f32[128,128]{0,1:T(8,128)}), (f32[128,1280]{1,0:T(8,128)}, f32[128,128]{0,1:T(8,128)})) %all-reduce.11.cloned.1.call-update) | async-done | bytes 720912 | tf_op jit(solution)/shard_map/psum | solution.py:25
  292.4 0.9 copy.16
  293.4 0.9 fusion.6
  294.2 11.7 %cholesky.55 = f32[128,128]{1,0:T(8,128)S(1)} custom-call(f32[128,128]{1,0:T(8,128)S(1)} %fusion.6), custom_call_target="Cholesky" | custom-call | tf_op jit(solution)/shard_map/jit(cholesky)/cholesky | solution.py:26
  307.3 9.8 %custom-call.13 = f32[1,128,128]{1,2,0:T(8,128)S(1)} custom-call(f32[1,128,128]{2,1,0:T(8,128)S(1)} %fusion.1), custom_call_target="InvertDiagBlocksLowerTriangular" | custom-call | tf_op jit(solution)/shard_map/jit(_solve_triangular)/triangular_solve | solution.py:28
  317.1 1.8 fusion.2
  318.9 0.7 fusion.4
  319.7 7.9 %convolution_subtract_fusion = f32[1024,1280]{1,0:T(8,128)} fusion(f32[1024,1280]{1,0:T(8,128)} %copy-done, f32[1024,128]{1,0:T(8,128)S(1)} %copy-done.2, f32[128,1280]{1,0:T(8,128)S(1)} %fusion.4), kind=kOutput, calls=%fused_computation | convolution fusion | flops 2014576640 | bytes 11665408 | tf_op jit(solution)/shard_map/dot_general | solution.py:15
  327.6 5.9 %copy.17 = f32[1024,1280]{0,1:T(8,128)} copy(f32[1024,1280]{1,0:T(8,128)} %convolution_subtract_fusion) | data formatting | bytes 10485760 | tf_op jit(solution)/shard_map/sub | solution.py:29
  333.6 5.9 %copy.19 = f32[1024,10,128]{2,0,1:T(8,128)} copy(f32[1024,10,128]{0,2,1:T(8,128)} %bitcast.47) | data formatting | bytes 10485760
  339.4 1.5 copy.18
  340.9 2.8 copy.20
  (19 shorter events, 2.7 us)
Async XLA Ops:
  7.2 47.0 %all-reduce.7.cloned.1.call-start = ((), (), s32[]{:S(2)}) async-start(), calls=%async_computation | async-start | bytes 1048576 | tf_op jit(solution)/shard_map/psum | solution.py:11
  20.9 118.6 %all-reduce.13.cloned.1.call-start = ((), (), s32[]{:S(2)}) async-start(), calls=%async_computation.3 | async-start | bytes 1441792 | tf_op jit(solution)/shard_map/psum | solution.py:25
  54.2 8.0 %copy-start.1 = (f32[1024,128]{1,0:T(8,128)S(1)}, f32[1024,128]{1,0:T(8,128)}, u32[]{:S(2)}) copy-start(f32[1024,128]{1,0:T(8,128)} %all-reduce.7.cloned.1.call-done) | copy-start | bytes 1572868
  63.8 143.6 %all-reduce.9.cloned.1.call-start = ((), (), s32[]{:S(2)}) async-start(), calls=%async_computation.1 | async-start | bytes 1048576 | tf_op jit(solution)/shard_map/psum | solution.py:11
  173.1 2.4 copy-start
  176.3 116.1 %all-reduce.11.cloned.1.call-start = ((), (), s32[]{:S(2)}) async-start(), calls=%async_computation.2 | async-start | bytes 1441792 | tf_op jit(solution)/shard_map/psum | solution.py:25
  210.3 109.4 %copy-start.2 = (f32[1024,128]{1,0:T(8,128)S(1)}, f32[1024,128]{1,0:T(8,128)}, u32[]{:S(2)}) copy-start(f32[1024,128]{1,0:T(8,128)} %all-reduce.9.cloned.1.call-done) | copy-start | bytes 1572868
Sparse Core Ops, SparseCore 0:
  21.1 33.0 all-reduce.6
  63.9 75.5 all-reduce.12
  176.4 30.9 all-reduce.8
  216.8 75.5 all-reduce.10
where the time goes:
time: 353 us; the launch traced here: 350 us
  waiting for transfers between devices  215 us (61%)
  other arithmetic  50.2 us (14%)
  matrix products  38.1 us (11%)
  local copies, waits for them, and re-layouts  32.1 us (9%)
  between operations  13.9 us (4%)
    psum x2, waiting for transfers between devices, factor(): gram_block, cross_terms = lax.psum((gram_block, cross_terms), 'rows')  151 us
    psum x2, waiting for transfers between devices, spread(): return lax.psum(block, axis)  64 us
    dot_general x6, matrix products, product(): jnp.dot(left, right, precision=PRECISE, preferred_element_type=jnp.float32)  33.1 us
    another operation x6, other arithmetic, factor(): triangle = jnp.linalg.cholesky(gram_block)  24.8 us
    another operation x4, other arithmetic, factor(): jax.scipy.linalg.solve_triangular(triangle, weights, trans=1, lower=True)  20.9 us
    unnamed x9, local copies, waits for them, and re-layouts  16.9 us
  transfers between devices with their start and end apart: 4, of which 4 were waited for; matrix products, arithmetic and copies ran while one was open for 0% of the time, Pallas kernels for 0%

commit v1 on v0

v1 whole, which is shorter than its diff:
```python
import functools

import jax
import jax.numpy as jnp
from jax import lax
from jax.experimental import pallas as pl
from jax.experimental.pallas import tpu as pltpu
from jax.sharding import PartitionSpec as P

PRECISE = lax.Precision.HIGHEST
MESH = pl.DeviceIdType.MESH
PIECES = 4
STRIP = 32


def product(left, right, contract):
    return lax.dot_general(
        left, right, ((contract[:1], contract[1:]), ((), ())),
        precision=PRECISE, preferred_element_type=jnp.float32)


def remote(src, dst, send, recv, row, col):
    return pltpu.make_async_remote_copy(
        src_ref=src, dst_ref=dst, send_sem=send, recv_sem=recv,
        device_id=(row, col), device_id_type=MESH)


def ring_place(index, n):
    z, y = index // 2, index % 2
    return jnp.where(y == 0, z, n - 1 - z)


def ring_row(place, n):
    place = lax.rem(place + n, n)
    return jnp.where(place < n // 2, 2 * place, 2 * (n - 1 - place) + 1)


def sums_kernel(n, chips, c_hbm, panels, total, columns, cross, slots,
                load_sem, own_sem, x_send, x_recv, d_send, d_recv, rs_send, rs_recv, ag_send, ag_recv):
    row, col = lax.axis_index("rows"), lax.axis_index("cols")
    chip, core = col // 2, col % 2
    sibling = chip * 2 + 1 - core
    place = ring_place(row, n)
    ahead, behind = ring_row(place + 1, n), ring_row(place - 1, n)
    rounds, rows_dev, blk = columns.shape
    piece = rows_dev // PIECES

    loads = [pltpu.make_async_copy(c_hbm.at[r], columns.at[r], load_sem.at[r]) for r in range(rounds)]
    for load in loads:
        load.start()

    barrier = pltpu.get_barrier_semaphore()
    for to in (ahead, behind):
        pl.semaphore_signal(barrier, inc=1, device_id=(to, col), device_id_type=MESH)
    pl.semaphore_signal(barrier, inc=1, device_id=(row, sibling), device_id_type=MESH)

    @pl.when(chip > 0)
    def _():
        pl.semaphore_signal(barrier, inc=1, device_id=(row, col - 2), device_id_type=MESH)

    @pl.when(chip < chips - 1)
    def _():
        pl.semaphore_signal(barrier, inc=1, device_id=(row, col + 2), device_id_type=MESH)

    expected = 3 + jnp.where(chip > 0, 1, 0) + jnp.where(chip < chips - 1, 1, 0)
    pl.semaphore_wait(barrier, expected)

    def part(which, at):
        return panels.at[which, pl.ds(at * piece, piece)]

    def along(at):
        return remote(part(core, at), part(core, at), x_send.at[at], x_recv.at[at], row, col + 2)

    def across(at):
        return remote(part(core, at), part(core, at), d_send.at[at], d_recv.at[at], row, sibling)

    def from_sibling(at):
        return remote(part(1 - core, at), part(1 - core, at), d_send.at[at], d_recv.at[at], row, sibling)

    @pl.when(chip == 0)
    def _():
        own = [pltpu.make_async_copy(c_hbm.at[0, pl.ds(at * piece, piece)], part(core, at), own_sem.at[at])
               for at in range(PIECES)]
        for copy in own:
            copy.start()
        for copy in own:
            copy.wait()

    for load in loads:
        load.wait()

    for at in range(PIECES):
        @pl.when(chip > 0)
        def _():
            along(at).wait_recv()

        @pl.when(chip < chips - 1)
        def _():
            along(at).start()

        across(at).start()
        from_sibling(at).wait_recv()
        rows = pl.ds(at * piece, piece)
        both = jnp.concatenate([panels[0, rows, :], panels[1, rows, :]], axis=1)
        for r in range(0, rounds + 2, 2):
            if r < rounds:
                right = jnp.concatenate([columns[r, rows, :], columns[r + 1, rows, :]], axis=1)
            else:
                right = both
            term = product(both, right, (0, 0))
            if at > 0:
                cross[r] += term[:, :blk]
                cross[r + 1] += term[:, blk:]
            else:
                cross[r] = term[:, :blk]
                cross[r + 1] = term[:, blk:]

    height = cross.shape[1] // n
    third = (rounds + 2) // 4
    chains = [(0, 1), (third, 1), (2 * third, -1), (3 * third, -1)]

    def chunk(way, back):
        at = lax.rem(place - way * back + 4 * n, n)
        return pl.ds(pl.multiple_of(at * height, height), height)

    def target(way):
        return ahead if way > 0 else behind

    sums = {}
    gathers = {}
    for step in range(n):
        for which, (first, way) in enumerate(chains):
            over = pl.ds(first, third)
            rows = chunk(way, step)
            if step > 0:
                sums[which, step - 1].wait_recv()
            if step == 0:
                source = cross.at[over, rows]
            elif step < n - 1:
                slots[step - 1, over] += cross[over, rows, :]
                source = slots.at[step - 1, over]
            else:
                total[over, rows, :] = slots[step - 1, over] + cross[over, rows, :]
            if step < n - 1:
                copy = remote(source, slots.at[step, over], rs_send.at[which, step],
                              rs_recv.at[which, step], target(way), col)
                copy.start()
                sums[which, step] = copy
    for step in range(n):
        for which, (first, way) in enumerate(chains):
            over = pl.ds(first, third)
            rows = chunk(way, step - 1)
            if step > 0:
                arrived = total.at[over, rows]
                remote(arrived, arrived, ag_send.at[which, step - 1], ag_recv.at[which, step - 1],
                       target(way), col).wait_recv()
            if step < n - 1:
                copy = remote(total.at[over, rows], total.at[over, rows], ag_send.at[which, step],
                              ag_recv.at[which, step], target(way), col)
                copy.start()
                gathers[which, step] = copy
    for copy in sums.values():
        copy.wait_send()
    for copy in gathers.values():
        copy.wait_send()
    for at in range(PIECES):
        across(at).wait_send()

        @pl.when(chip < chips - 1)
        def _():
            along(at).wait_send()


def sums(block, n, chips):
    rounds, rows_dev, blk = block.shape
    wide = 2 * blk
    shape = jax.ShapeDtypeStruct
    dma = pltpu.SemaphoreType.DMA
    vmem = pl.BlockSpec(memory_space=pltpu.VMEM)
    return pl.pallas_call(
        functools.partial(sums_kernel, n, chips),
        out_shape=(shape((2, rows_dev, blk), jnp.float32), shape((rounds + 2, wide, blk), jnp.float32)),
        in_specs=[pl.BlockSpec(memory_space=pl.ANY)],
        out_specs=(vmem, vmem),
        scratch_shapes=[
            pltpu.VMEM((rounds, rows_dev, blk), jnp.float32),
            pltpu.VMEM((rounds + 2, wide, blk), jnp.float32),
            pltpu.VMEM((n - 1, rounds + 2, wide // n, blk), jnp.float32),
            dma((rounds,)), dma((PIECES,)), dma((PIECES,)), dma((PIECES,)), dma((PIECES,)), dma((PIECES,)),
            dma((4, n - 1)), dma((4, n - 1)), dma((4, n - 1)), dma((4, n - 1)),
        ],
        compiler_params=pltpu.CompilerParams(
            collective_id=0, has_side_effects=True, vmem_limit_bytes=48 * 2**20),
        name="panel_sums",
    )(block)


def eliminate(work, inverse):
    wide = inverse.shape[0]
    for top in range(0, wide, STRIP):
        strip = work[top:top + STRIP, :]
        down = lax.broadcasted_iota(jnp.int32, (STRIP, 1), 0)
        scale = jnp.ones((STRIP, 1), jnp.float32)
        for j in range(STRIP):
            column = strip[:, top + j:top + j + 1]
            pivot = column[j:j + 1, :]
            scale = jnp.where(down == j, lax.rsqrt(pivot), scale)
            if j < STRIP - 1:
                factors = jnp.where(down > j, column * (1.0 / pivot), 0.0)
                strip = strip - factors * strip[j:j + 1, :]
        strip = strip * scale
        inverse[top:top + STRIP, :] = strip[:, wide:]
        if top + STRIP < wide:
            below = strip[:, :wide]
            work[...] -= product(below, strip, (0, 0))


def reduce_kernel(sums_ref, panels, c_ref, reduced, top_rows, work, inverse):
    rounds = sums_ref.shape[0] - 2
    blk = c_ref.shape[2]
    wide = 2 * blk
    step = pl.program_id(0)

    @pl.when(step == 0)
    def _():
        work[:, :blk] = sums_ref[rounds]
        work[:, blk:wide] = sums_ref[rounds + 1]
        across = lax.broadcasted_iota(jnp.int32, (wide, wide), 1)
        down = lax.broadcasted_iota(jnp.int32, (wide, wide), 0)
        work[:, wide:] = jnp.where(across == down, 1.0, 0.0).astype(jnp.float32)
        eliminate(work, inverse)

    cross = jnp.concatenate([sums_ref[2 * step], sums_ref[2 * step + 1]], axis=1)
    weights = product(inverse[...], cross, (1, 0))
    top_rows[0] = weights[:, :blk]
    top_rows[1] = weights[:, blk:]
    coefficients = product(inverse[...], weights, (0, 0))
    both = jnp.concatenate([panels[0], panels[1]], axis=1)
    span = product(both, coefficients, (1, 0))
    reduced[0] = c_ref[0] - span[:, :blk]
    reduced[1] = c_ref[1] - span[:, blk:]


def reduce(total, panels, block):
    rounds, rows_dev, blk = block.shape
    wide = 2 * blk
    shape = jax.ShapeDtypeStruct
    whole = lambda array: pl.BlockSpec(array.shape, lambda i: (0, 0, 0))
    pair = pl.BlockSpec((2, rows_dev, blk), lambda i: (i, 0, 0))
    return pl.pallas_call(
        reduce_kernel,
        grid=(rounds // 2,),
        out_shape=(shape(block.shape, jnp.float32), shape((rounds, wide, blk), jnp.float32)),
        in_specs=[whole(total), whole(panels), pair],
        out_specs=(pair, pl.BlockSpec((2, wide, blk), lambda i: (i, 0, 0))),
        scratch_shapes=[pltpu.VMEM((wide, 2 * wide), jnp.float32), pltpu.VMEM((wide, wide), jnp.float32)],
        compiler_params=pltpu.CompilerParams(vmem_limit_bytes=48 * 2**20),
        name="reduce_columns",
    )(total, panels, block)


def solution(mesh):
    n, chips = mesh.shape["rows"], mesh.shape["cols"] // 2

    def shards(matrix):
        block = jnp.transpose(matrix, (1, 0, 2))
        panels, total = sums(block, n, chips)
        reduced, top_rows = reduce(total, panels, block)
        return jnp.transpose(reduced, (1, 0, 2)), jnp.transpose(top_rows, (1, 0, 2))

    return jax.shard_map(
        shards,
        mesh=mesh,
        in_specs=(P("rows", None, "cols"),),
        out_specs=(P("rows", None, "cols"), P(None, None, "cols")),
        check_vma=False,
    )
```

time: 353 us -> 111 us (0.31)
  waiting for transfers between devices: 215 us -> 0 us
  Pallas kernels: 0 us -> 111 us
  other arithmetic: 50.2 us -> 0 us
  matrix products: 38.1 us -> 0 us
  local copies, waits for them, and re-layouts: 32.1 us -> 0 us
  between operations: 13.9 us -> 0.64 us
    psum x4 -> x0, waiting for transfers between devices: 215 us -> none  [the longest x2 151 us: factor(): gram_block, cross_terms = lax.psum((gram_block, cross_terms), 'rows')]
    pallas_call x0 -> x2, Pallas kernels: none -> 111 us  [the longest x1 72 us: sums(): pl.pallas_call(functools.partial(sums_kernel, n, chips), out_shape=(shape...]
    another operation x10 -> x0, other arithmetic: 45.7 us -> none  [the longest x6 24.8 us: factor(): triangle = jnp.linalg.cholesky(gram_block)]
    dot_general x6 -> x0, matrix products: 33.1 us -> none  [product(): jnp.dot(left, right, precision=PRECISE, preferred_element_type=jnp.float32)]
    unnamed x9 -> x0, local copies, waits for them, and re-layouts: 16.9 us -> none
    sub x1 -> x0, local copies, waits for them, and re-layouts: 5.93 us -> none  [factor(): return (weights, columns - product(panel, coefficients))]
    reshape x1 -> x0, local copies, waits for them, and re-layouts: 5.92 us -> none  [shards(): columns = matrix.reshape(rows_dev, rounds * width)]
    another operation x4 -> x0, matrix products: 4.96 us -> none  [the longest x2 3.61 us: factor(): jax.scipy.linalg.solve_triangular(triangle, cross_terms, lower=True)]
  transfers between devices with their start and end apart: 4 -> 0, of which waited for: 4 -> 0; matrix products, arithmetic and copies ran while one was open for 0% -> 0% of each run, Pallas kernels for 0% -> 0%
where the time goes in v1:
time: 111 us
  Pallas kernels  111 us (100%)
    pallas_call x1, Pallas kernels, sums(): pl.pallas_call(functools.partial(sums_kernel, n, chips), out_shape=(shape...  72 us
    pallas_call x1, Pallas kernels, reduce(): pl.pallas_call(reduce_kernel, grid=(rounds // 2,), out_shape=(shape(block...  38.6 us

profile of v1, /device:TPU:2, one launch (start us, length us, event | category | flops | bytes accessed | tf_op | source)
XLA Modules:
  0.0 111.3 jit_solution(779072989770113247)
XLA Ops:
  0.6 72.0 %panel_sums.1 = (f32[2,1024,128]{2,1,0:T(8,128)S(1)}, f32[12,256,128]{2,1,0:T(8,128)S(1)}) custom-call(f32[10,1024,128]{2,1,0:T(8,128)} %bitcast.3), custom_call_target="tpu_custom_call" | custom-call | tf_op jit(solution)/shard_map/panel_sums/pallas_call | solution.py:180
  72.7 38.6 %reduce_columns.1 = (f32[10,1024,128]{2,1,0:T(8,128)}, f32[10,256,128]{2,1,0:T(8,128)}) custom-call(f32[12,256,128]{2,1,0:T(8,128)S(1)} %get-tuple-element.6.sums_ref, f32[2,1024,128]{2,1,0:T(8,128)S(1)} %get-tuple-element.7.panels, f32[10,1024,128]{2,1,0:T(8,128)} %bitcast.4), custom_call_target="tpu_custom_call" | custom-call | tf_op jit(solution)/shard_map/reduce_columns/pallas_call | solution.py:250

commit v2 on v1

--- a/solution.py
+++ b/solution.py
@@ -19,6 +19,16 @@
         precision=PRECISE, preferred_element_type=jnp.float32)
 
 
+def split(value):
+    high = value.astype(jnp.bfloat16)
+    return high, (value - high.astype(jnp.float32)).astype(jnp.bfloat16)
+
+
+def split_product(left, right):
+    dot = functools.partial(jnp.dot, preferred_element_type=jnp.float32)
+    return dot(left[0], right[0]) + (dot(left[0], right[1]) + dot(left[1], right[0]))
+
+
 def remote(src, dst, send, recv, row, col):
     return pltpu.make_async_remote_copy(
         src_ref=src, dst_ref=dst, send_sem=send, recv_sem=recv,
@@ -35,8 +45,8 @@
     return jnp.where(place < n // 2, 2 * place, 2 * (n - 1 - place) + 1)
 
 
-def sums_kernel(n, chips, c_hbm, panels, total, columns, cross, slots,
-                load_sem, own_sem, x_send, x_recv, d_send, d_recv, rs_send, rs_recv, ag_send, ag_recv):
+def sums_kernel(n, chips, c_hbm, panels, total, inverse, columns, cross, slots, gram, inbox, mine, other, work,
+                gs_send, gs_recv, gg_send, gg_recv, half_send, half_recv, load_sem, own_sem, x_send, x_recv, d_send, d_recv, rs_send, rs_recv, ag_send, ag_recv):
     row, col = lax.axis_index("rows"), lax.axis_index("cols")
     chip, core = col // 2, col % 2
     sibling = chip * 2 + 1 - core
@@ -50,8 +60,8 @@
         load.start()
 
     barrier = pltpu.get_barrier_semaphore()
-    for to in (ahead, behind):
-        pl.semaphore_signal(barrier, inc=1, device_id=(to, col), device_id_type=MESH)
+    for far in range(1, n):
+        pl.semaphore_signal(barrier, inc=1, device_id=(lax.rem(row + far, n), col), device_id_type=MESH)
     pl.semaphore_signal(barrier, inc=1, device_id=(row, sibling), device_id_type=MESH)
 
     @pl.when(chip > 0)
@@ -62,7 +72,7 @@
     def _():
         pl.semaphore_signal(barrier, inc=1, device_id=(row, col + 2), device_id_type=MESH)
 
-    expected = 3 + jnp.where(chip > 0, 1, 0) + jnp.where(chip < chips - 1, 1, 0)
+    expected = n + jnp.where(chip > 0, 1, 0) + jnp.where(chip < chips - 1, 1, 0)
     pl.semaphore_wait(barrier, expected)
 
     def part(which, at):
@@ -89,6 +99,72 @@
     for load in loads:
         load.wait()
 
+    owners = min(n, blk // 8)
+    share = blk // owners
+
+    def owned(owner):
+        return pl.ds(pl.multiple_of(core * blk + owner * share, 8), share)
+
+    def kept(owner):
+        return pl.ds(pl.multiple_of(owner * share, 8), share)
+
+    def only(condition, run):
+        if owners == n:
+            run()
+        else:
+            pl.when(condition)(run)
+
+    def peer(far):
+        return lax.rem(row + far, n)
+
+    def scattered(far):
+        return remote(gram.at[owned(lax.rem(peer(far), owners))], inbox.at[far - 1], gs_send.at[far - 1],
+                      gs_recv.at[far - 1], peer(far), col)
+
+    def gathered(far, owner):
+        return remote(mine.at[kept(owner)], mine.at[kept(owner)], gg_send.at[far - 1],
+                      gg_recv.at[far - 1], peer(far), col)
+
+    def half(which):
+        return pl.ds(pl.multiple_of(which * blk, blk), blk)
+
+    def halved():
+        return remote(mine, other, half_send.at[0], half_recv.at[0], row, sibling)
+
+    def scatter_gram():
+        for far in range(1, n):
+            only(peer(far) < owners, lambda: scattered(far).start())
+
+    def gather_gram():
+        for far in range(1, n):
+            only(peer(far) < owners, lambda: scattered(far).wait_send())
+
+        def add():
+            for far in range(1, n):
+                scattered(far).wait_recv()
+            summed = gram[owned(lax.rem(row, owners)), :]
+            for far in range(1, n):
+                summed = summed + inbox[far - 1]
+            mine[kept(lax.rem(row, owners)), :] = summed
+            for far in range(1, n):
+                gathered(far, lax.rem(row, owners)).start()
+
+        only(row < owners, add)
+
+    def swap_gram():
+        for far in range(1, n):
+            sender = lax.rem(row + n - far, n)
+            only(sender < owners, lambda: gathered(far, lax.rem(sender, owners)).wait_recv())
+        halved().start()
+
+    def place_gram():
+        halved().wait_recv()
+        across_ = lax.broadcasted_iota(jnp.int32, gram.shape, 1)
+        down = lax.broadcasted_iota(jnp.int32, gram.shape, 0)
+        work[half(core), :2 * blk] = mine[...]
+        work[half(1 - core), :2 * blk] = other[...]
+        work[:, 2 * blk:] = jnp.where(across_ == down, 1.0, 0.0).astype(jnp.float32)
+
     for at in range(PIECES):
         @pl.when(chip > 0)
         def _():
@@ -102,12 +178,14 @@
         from_sibling(at).wait_recv()
         rows = pl.ds(at * piece, piece)
         both = jnp.concatenate([panels[0, rows, :], panels[1, rows, :]], axis=1)
-        for r in range(0, rounds + 2, 2):
-            if r < rounds:
-                right = jnp.concatenate([columns[r, rows, :], columns[r + 1, rows, :]], axis=1)
-            else:
-                right = both
-            term = product(both, right, (0, 0))
+        term = product(both, both, (0, 0))
+        gram[...] = term if at == 0 else gram[...] + term
+        if at == PIECES - 1:
+            scatter_gram()
+        flipped = split(both.T)
+        for r in range(0, rounds, 2):
+            right = jnp.concatenate([columns[r, rows, :], columns[r + 1, rows, :]], axis=1)
+            term = split_product(flipped, split(right))
             if at > 0:
                 cross[r] += term[:, :blk]
                 cross[r + 1] += term[:, blk:]
@@ -116,8 +194,9 @@
                 cross[r + 1] = term[:, blk:]
 
     height = cross.shape[1] // n
-    third = (rounds + 2) // 4
-    chains = [(0, 1), (third, 1), (2 * third, -1), (3 * third, -1)]
+    most, least = (rounds + 2) // 4, rounds // 2 - (rounds + 2) // 4
+    chains = [(0, most, 1), (most, least, 1), (rounds // 2, most, -1), (rounds // 2 + most, least, -1)]
+    items = eliminate(work, inverse)
 
     def chunk(way, back):
         at = lax.rem(place - way * back + 4 * n, n)
@@ -129,8 +208,8 @@
     sums = {}
     gathers = {}
     for step in range(n):
-        for which, (first, way) in enumerate(chains):
-            over = pl.ds(first, third)
+        for which, (first, count, way) in enumerate(chains):
+            over = pl.ds(first, count)
             rows = chunk(way, step)
             if step > 0:
                 sums[which, step - 1].wait_recv()
@@ -146,9 +225,17 @@
                               rs_recv.at[which, step], target(way), col)
                 copy.start()
                 sums[which, step] = copy
+            if step >= 3:
+                next(items, None)
+        if step == 0:
+            gather_gram()
+        elif step == 1:
+            swap_gram()
+        elif step == 2:
+            place_gram()
     for step in range(n):
-        for which, (first, way) in enumerate(chains):
-            over = pl.ds(first, third)
+        for which, (first, count, way) in enumerate(chains):
+            over = pl.ds(first, count)
             rows = chunk(way, step - 1)
             if step > 0:
                 arrived = total.at[over, rows]
@@ -159,6 +246,11 @@
                               ag_recv.at[which, step], target(way), col)
                 copy.start()
                 gathers[which, step] = copy
+            next(items, None)
+    for item in items:
+        pass
+    halved().wait_send()
+    only(row < owners, lambda: [gathered(far, lax.rem(row, owners)).wait_send() for far in range(1, n)] and None)
     for copy in sums.values():
         copy.wait_send()
     for copy in gathers.values():
@@ -179,13 +271,20 @@
     vmem = pl.BlockSpec(memory_space=pltpu.VMEM)
     return pl.pallas_call(
         functools.partial(sums_kernel, n, chips),
-        out_shape=(shape((2, rows_dev, blk), jnp.float32), shape((rounds + 2, wide, blk), jnp.float32)),
+        out_shape=(shape((2, rows_dev, blk), jnp.float32), shape((rounds, wide, blk), jnp.float32),
+                   shape((wide, wide), jnp.float32)),
         in_specs=[pl.BlockSpec(memory_space=pl.ANY)],
-        out_specs=(vmem, vmem),
+        out_specs=(vmem, vmem, vmem),
         scratch_shapes=[
             pltpu.VMEM((rounds, rows_dev, blk), jnp.float32),
-            pltpu.VMEM((rounds + 2, wide, blk), jnp.float32),
-            pltpu.VMEM((n - 1, rounds + 2, wide // n, blk), jnp.float32),
+            pltpu.VMEM((rounds, wide, blk), jnp.float32),
+            pltpu.VMEM((n - 1, rounds, wide // n, blk), jnp.float32),
+            pltpu.VMEM((wide, wide), jnp.float32),
+            pltpu.VMEM((n - 1, blk // min(n, blk // 8), wide), jnp.float32),
+            pltpu.VMEM((blk, wide), jnp.float32),
+            pltpu.VMEM((blk, wide), jnp.float32),
+            pltpu.VMEM((wide, 2 * wide), jnp.float32),
+            dma((n - 1,)), dma((n - 1,)), dma((n - 1,)), dma((n - 1,)), dma((1,)), dma((1,)),
             dma((rounds,)), dma((PIECES,)), dma((PIECES,)), dma((PIECES,)), dma((PIECES,)), dma((PIECES,)),
             dma((4, n - 1)), dma((4, n - 1)), dma((4, n - 1)), dma((4, n - 1)),
         ],
@@ -208,55 +307,50 @@
             if j < STRIP - 1:
                 factors = jnp.where(down > j, column * (1.0 / pivot), 0.0)
                 strip = strip - factors * strip[j:j + 1, :]
+            if j % 8 == 7 and j < STRIP - 1:
+                yield
         strip = strip * scale
         inverse[top:top + STRIP, :] = strip[:, wide:]
         if top + STRIP < wide:
             below = strip[:, :wide]
             work[...] -= product(below, strip, (0, 0))
-
-
-def reduce_kernel(sums_ref, panels, c_ref, reduced, top_rows, work, inverse):
-    rounds = sums_ref.shape[0] - 2
+        yield
+
+
+def reduce_kernel(sums_ref, inverse, panels, c_ref, reduced, top_rows, high, low):
     blk = c_ref.shape[2]
-    wide = 2 * blk
     step = pl.program_id(0)
 
     @pl.when(step == 0)
     def _():
-        work[:, :blk] = sums_ref[rounds]
-        work[:, blk:wide] = sums_ref[rounds + 1]
-        across = lax.broadcasted_iota(jnp.int32, (wide, wide), 1)
-        down = lax.broadcasted_iota(jnp.int32, (wide, wide), 0)
-        work[:, wide:] = jnp.where(across == down, 1.0, 0.0).astype(jnp.float32)
-        eliminate(work, inverse)
+        high[...], low[...] = split(jnp.concatenate([panels[0], panels[1]], axis=1))
 
     cross = jnp.concatenate([sums_ref[2 * step], sums_ref[2 * step + 1]], axis=1)
     weights = product(inverse[...], cross, (1, 0))
     top_rows[0] = weights[:, :blk]
     top_rows[1] = weights[:, blk:]
     coefficients = product(inverse[...], weights, (0, 0))
-    both = jnp.concatenate([panels[0], panels[1]], axis=1)
-    span = product(both, coefficients, (1, 0))
+    span = split_product((high[...], low[...]), split(coefficients))
     reduced[0] = c_ref[0] - span[:, :blk]
     reduced[1] = c_ref[1] - span[:, blk:]
 
 
-def reduce(total, panels, block):
+def reduce(total, inverse, panels, block):
     rounds, rows_dev, blk = block.shape
     wide = 2 * blk
     shape = jax.ShapeDtypeStruct
-    whole = lambda array: pl.BlockSpec(array.shape, lambda i: (0, 0, 0))
+    whole = lambda array: pl.BlockSpec(array.shape, lambda i: (0,) * len(array.shape))
     pair = pl.BlockSpec((2, rows_dev, blk), lambda i: (i, 0, 0))
     return pl.pallas_call(
         reduce_kernel,
         grid=(rounds // 2,),
         out_shape=(shape(block.shape, jnp.float32), shape((rounds, wide, blk), jnp.float32)),
-        in_specs=[whole(total), whole(panels), pair],
+        in_specs=[whole(total), whole(inverse), whole(panels), pair],
         out_specs=(pair, pl.BlockSpec((2, wide, blk), lambda i: (i, 0, 0))),
-        scratch_shapes=[pltpu.VMEM((wide, 2 * wide), jnp.float32), pltpu.VMEM((wide, wide), jnp.float32)],
+        scratch_shapes=[pltpu.VMEM((rows_dev, wide), jnp.bfloat16)] * 2,
         compiler_params=pltpu.CompilerParams(vmem_limit_bytes=48 * 2**20),
         name="reduce_columns",
-    )(total, panels, block)
+    )(total, inverse, panels, block)
 
 
 def solution(mesh):
@@ -264,8 +358,8 @@
 
     def shards(matrix):
         block = jnp.transpose(matrix, (1, 0, 2))
-        panels, total = sums(block, n, chips)
-        reduced, top_rows = reduce(total, panels, block)
+        panels, total, inverse = sums(block, n, chips)
+        reduced, top_rows = reduce(total, inverse, panels, block)
         return jnp.transpose(reduced, (1, 0, 2)), jnp.transpose(top_rows, (1, 0, 2))
 
     return jax.shard_map(

time: 111 us -> 91.5 us (0.82)
  Pallas kernels: 111 us -> 90.6 us
    pallas_call x1, Pallas kernels: 38.6 us -> 10.6 us  [reduce(): pl.pallas_call(reduce_kernel, grid=(rounds // 2,), out_shape=(shape(block...]
    pallas_call x1, Pallas kernels: 72 us -> 79.9 us  [sums(): pl.pallas_call(functools.partial(sums_kernel, n, chips), out_shape=(shape...]
where the time goes in v2:
time: 91.5 us; the launch traced here: 91.2 us
  Pallas kernels  90.6 us (99%)
    pallas_call x1, Pallas kernels, sums(): pl.pallas_call(functools.partial(sums_kernel, n, chips), out_shape=(shape...  79.9 us
    pallas_call x1, Pallas kernels, reduce(): pl.pallas_call(reduce_kernel, grid=(rounds // 2,), out_shape=(shape(block...  10.6 us

profile of v2, /device:TPU:2, one launch (start us, length us, event | category | flops | bytes accessed | tf_op | source)
XLA Modules:
  0.0 91.2 jit_solution(9053616655627047845)
XLA Ops:
  0.6 79.9 %panel_sums.1 = (f32[2,1024,128]{2,1,0:T(8,128)S(1)}, f32[10,256,128]{2,1,0:T(8,128)S(1)}, f32[256,256]{1,0:T(8,128)S(1)}) custom-call(f32[10,1024,128]{2,1,0:T(8,128)} %bitcast.3), custom_call_target="tpu_custom_call" | custom-call | tf_op jit(solution)/shard_map/panel_sums/pallas_call | solution.py:272
  80.6 10.6 %reduce_columns.1 = (f32[10,1024,128]{2,1,0:T(8,128)}, f32[10,256,128]{2,1,0:T(8,128)}) custom-call(f32[10,256,128]{2,1,0:T(8,128)S(1)} %get-tuple-element.7.sums_ref, f32[256,256]{1,0:T(8,128)S(1)} %get-tuple-element.8.inverse, f32[2,1024,128]{2,1,0:T(8,128)S(1)} %get-tuple-element.9.panels, f32[10,1024,128]{2,1,0:T(8,128)} %bitcast.4), custom_call_target="tpu_custom_call" | custom-call | tf_op jit(solution)/shard_map/reduce_columns/pallas_call | solution.py:344

commit v3 on v2

--- a/solution.py
+++ b/solution.py
@@ -35,23 +35,11 @@
         device_id=(row, col), device_id_type=MESH)
 
 
-def ring_place(index, n):
-    z, y = index // 2, index % 2
-    return jnp.where(y == 0, z, n - 1 - z)
-
-
-def ring_row(place, n):
-    place = lax.rem(place + n, n)
-    return jnp.where(place < n // 2, 2 * place, 2 * (n - 1 - place) + 1)
-
-
 def sums_kernel(n, chips, c_hbm, panels, total, inverse, columns, cross, slots, gram, inbox, mine, other, work,
                 gs_send, gs_recv, gg_send, gg_recv, half_send, half_recv, load_sem, own_sem, x_send, x_recv, d_send, d_recv, rs_send, rs_recv, ag_send, ag_recv):
     row, col = lax.axis_index("rows"), lax.axis_index("cols")
     chip, core = col // 2, col % 2
     sibling = chip * 2 + 1 - core
-    place = ring_place(row, n)
-    ahead, behind = ring_row(place + 1, n), ring_row(place - 1, n)
     rounds, rows_dev, blk = columns.shape
     piece = rows_dev // PIECES
 
@@ -193,68 +181,74 @@
                 cross[r] = term[:, :blk]
                 cross[r + 1] = term[:, blk:]
 
-    height = cross.shape[1] // n
-    most, least = (rounds + 2) // 4, rounds // 2 - (rounds + 2) // 4
-    chains = [(0, most, 1), (most, least, 1), (rounds // 2, most, -1), (rounds // 2 + most, least, -1)]
+    wide = 2 * blk
+    bits = n.bit_length() - 1
+    plain = list(range(bits))
+    swapped = [1, 0] + plain[2:] if bits > 1 else plain
+    chains = [(first, plain if first % 4 == 0 else swapped) for first in range(0, rounds, 2)]
     items = eliminate(work, inverse)
 
-    def chunk(way, back):
-        at = lax.rem(place - way * back + 4 * n, n)
-        return pl.ds(pl.multiple_of(at * height, height), height)
-
-    def target(way):
-        return ahead if way > 0 else behind
-
-    sums = {}
-    gathers = {}
-    for step in range(n):
-        for which, (first, count, way) in enumerate(chains):
-            over = pl.ds(first, count)
-            rows = chunk(way, step)
-            if step > 0:
-                sums[which, step - 1].wait_recv()
-            if step == 0:
-                source = cross.at[over, rows]
-            elif step < n - 1:
-                slots[step - 1, over] += cross[over, rows, :]
-                source = slots.at[step - 1, over]
+    def side(bit):
+        return (row // 2 ** bit) % 2
+
+    def partner(bit):
+        return row + (1 - 2 * side(bit)) * 2 ** bit
+
+    def start_of(order, phases):
+        at = 0
+        for t in range(phases):
+            at = at + side(order[t]) * (wide >> (t + 1))
+        return at
+
+    def span_of(at, size):
+        return pl.ds(pl.multiple_of(at, 8), size)
+
+    def halve(which, t):
+        first, order = chains[which]
+        over, size = pl.ds(first, 2), wide >> (t + 1)
+        sent = start_of(order, t) + (1 - side(order[t])) * size
+        return remote(cross.at[over, span_of(sent, size)], slots.at[over, pl.ds(wide - 2 * size, size)],
+                      rs_send.at[which, t], rs_recv.at[which, t], partner(order[t]), col)
+
+    def double(which, t):
+        first, order = chains[which]
+        size = wide >> (t + 1)
+        held = total.at[pl.ds(first, 2), span_of(start_of(order, t + 1), size)]
+        return remote(held, held, ag_send.at[which, t], ag_recv.at[which, t], partner(order[t]), col)
+
+    def add(which, t):
+        first, order = chains[which]
+        over, size = pl.ds(first, 2), wide >> (t + 1)
+        kept_rows = span_of(start_of(order, t + 1), size)
+        into = total if t == bits - 1 else cross
+        into[over, kept_rows, :] = cross[over, kept_rows, :] + slots[over, pl.ds(wide - 2 * size, size), :]
+
+    early = [gather_gram, swap_gram, place_gram]
+    for which in range(len(chains)):
+        halve(which, 0).start()
+    for t in range(2 * bits):
+        for which in range(len(chains)):
+            if early:
+                early.pop(0)()
             else:
-                total[over, rows, :] = slots[step - 1, over] + cross[over, rows, :]
-            if step < n - 1:
-                copy = remote(source, slots.at[step, over], rs_send.at[which, step],
-                              rs_recv.at[which, step], target(way), col)
-                copy.start()
-                sums[which, step] = copy
-            if step >= 3:
                 next(items, None)
-        if step == 0:
-            gather_gram()
-        elif step == 1:
-            swap_gram()
-        elif step == 2:
-            place_gram()
-    for step in range(n):
-        for which, (first, count, way) in enumerate(chains):
-            over = pl.ds(first, count)
-            rows = chunk(way, step - 1)
-            if step > 0:
-                arrived = total.at[over, rows]
-                remote(arrived, arrived, ag_send.at[which, step - 1], ag_recv.at[which, step - 1],
-                       target(way), col).wait_recv()
-            if step < n - 1:
-                copy = remote(total.at[over, rows], total.at[over, rows], ag_send.at[which, step],
-                              ag_recv.at[which, step], target(way), col)
-                copy.start()
-                gathers[which, step] = copy
-            next(items, None)
+            if t < bits:
+                halve(which, t).wait_recv()
+                add(which, t)
+            else:
+                double(which, 2 * bits - 1 - t).wait_recv()
+            if t < bits - 1:
+                halve(which, t + 1).start()
+            elif t < 2 * bits - 1:
+                double(which, 2 * bits - 2 - t).start()
     for item in items:
         pass
     halved().wait_send()
     only(row < owners, lambda: [gathered(far, lax.rem(row, owners)).wait_send() for far in range(1, n)] and None)
-    for copy in sums.values():
-        copy.wait_send()
-    for copy in gathers.values():
-        copy.wait_send()
+    for which in range(len(chains)):
+        for t in range(bits):
+            halve(which, t).wait_send()
+            double(which, t).wait_send()
     for at in range(PIECES):
         across(at).wait_send()
 
@@ -278,7 +272,7 @@
         scratch_shapes=[
             pltpu.VMEM((rounds, rows_dev, blk), jnp.float32),
             pltpu.VMEM((rounds, wide, blk), jnp.float32),
-            pltpu.VMEM((n - 1, rounds, wide // n, blk), jnp.float32),
+            pltpu.VMEM((rounds, wide - wide // n, blk), jnp.float32),
             pltpu.VMEM((wide, wide), jnp.float32),
             pltpu.VMEM((n - 1, blk // min(n, blk // 8), wide), jnp.float32),
             pltpu.VMEM((blk, wide), jnp.float32),
@@ -286,7 +280,7 @@
             pltpu.VMEM((wide, 2 * wide), jnp.float32),
             dma((n - 1,)), dma((n - 1,)), dma((n - 1,)), dma((n - 1,)), dma((1,)), dma((1,)),
             dma((rounds,)), dma((PIECES,)), dma((PIECES,)), dma((PIECES,)), dma((PIECES,)), dma((PIECES,)),
-            dma((4, n - 1)), dma((4, n - 1)), dma((4, n - 1)), dma((4, n - 1)),
+            *[dma((rounds // 2, n.bit_length() - 1))] * 4,
         ],
         compiler_params=pltpu.CompilerParams(
             collective_id=0, has_side_effects=True, vmem_limit_bytes=48 * 2**20),
@@ -296,24 +290,40 @@
 
 def eliminate(work, inverse):
     wide = inverse.shape[0]
+    lanes = wide // 2
+    down = lax.broadcasted_iota(jnp.int32, (STRIP, lanes), 0)
+    inverse[:lanes, lanes:] = jnp.zeros((lanes, lanes), jnp.float32)
     for top in range(0, wide, STRIP):
-        strip = work[top:top + STRIP, :]
-        down = lax.broadcasted_iota(jnp.int32, (STRIP, 1), 0)
-        scale = jnp.ones((STRIP, 1), jnp.float32)
-        for j in range(STRIP):
-            column = strip[:, top + j:top + j + 1]
-            pivot = column[j:j + 1, :]
+        low = top // lanes
+        live = slice(low * lanes, low * lanes + 3 * lanes)
+        strip = work[top:top + STRIP, live]
+        scale = jnp.ones((STRIP, lanes), jnp.float32)
+        lane = top - low * lanes
+        for j in range(0, STRIP, 2):
+            first = jnp.broadcast_to(strip[:, lane + j:lane + j + 1], (STRIP, lanes))
+            second = jnp.broadcast_to(strip[:, lane + j + 1:lane + j + 2], (STRIP, lanes))
+            pivot = first[j:j + 1, :]
+            outer = jnp.where(down > j, first * (1.0 / pivot), 0.0)
+            second = second - outer * second[j:j + 1, :]
+            next_pivot = second[j + 1:j + 2, :]
+            inner = jnp.where(down > j + 1, second * (1.0 / next_pivot), 0.0)
             scale = jnp.where(down == j, lax.rsqrt(pivot), scale)
-            if j < STRIP - 1:
-                factors = jnp.where(down > j, column * (1.0 / pivot), 0.0)
-                strip = strip - factors * strip[j:j + 1, :]
-            if j % 8 == 7 and j < STRIP - 1:
+            scale = jnp.where(down == j + 1, lax.rsqrt(next_pivot), scale)
+            upper = strip[j:j + 1, :]
+            lower = strip[j + 1:j + 2, :] - jnp.concatenate([outer[j + 1:j + 2, :]] * 3, axis=1) * upper
+            strip = strip - (jnp.concatenate([outer] * 3, axis=1) * upper
+                             + jnp.concatenate([inner] * 3, axis=1) * lower)
+            if j % 8 == 6 and j < STRIP - 2:
                 yield
-        strip = strip * scale
-        inverse[top:top + STRIP, :] = strip[:, wide:]
+        strip = strip * jnp.concatenate([scale] * 3, axis=1)
+        if low == 0:
+            inverse[top:top + STRIP, :lanes] = strip[:, 2 * lanes:]
+        else:
+            inverse[top:top + STRIP, :] = strip[:, lanes:]
         if top + STRIP < wide:
-            below = strip[:, :wide]
-            work[...] -= product(below, strip, (0, 0))
+            above = (top + STRIP) // lanes * lanes
+            below = strip[:, above - low * lanes:wide - low * lanes]
+            work[above:, live] -= product(below, strip, (0, 0))
         yield
 
 

time: 91.5 us -> 78.9 us (0.86)
  Pallas kernels: 90.6 us -> 78 us
    pallas_call x1, Pallas kernels: 79.9 us -> 67.3 us  [sums(): pl.pallas_call(functools.partial(sums_kernel, n, chips), out_shape=(shape...]
where the time goes in v3:
time: 78.9 us; the launch traced here: 78.6 us
  Pallas kernels  78 us (99%)
    pallas_call x1, Pallas kernels, sums(): pl.pallas_call(functools.partial(sums_kernel, n, chips), out_shape=(shape...  67.3 us
    pallas_call x1, Pallas kernels, reduce(): pl.pallas_call(reduce_kernel, grid=(rounds // 2,), out_shape=(shape(block...  10.6 us

profile of v3, /device:TPU:2, one launch (start us, length us, event | category | flops | bytes accessed | tf_op | source)
XLA Modules:
  0.0 78.6 jit_solution(13579781443347600670)
XLA Ops:
  0.6 67.3 %panel_sums.1 = (f32[2,1024,128]{2,1,0:T(8,128)S(1)}, f32[10,256,128]{2,1,0:T(8,128)S(1)}, f32[256,256]{1,0:T(8,128)S(1)}) custom-call(f32[10,1024,128]{2,1,0:T(8,128)} %bitcast.3), custom_call_target="tpu_custom_call" | custom-call | tf_op jit(solution)/shard_map/panel_sums/pallas_call | solution.py:266
  68.0 10.6 %reduce_columns.1 = (f32[10,1024,128]{2,1,0:T(8,128)}, f32[10,256,128]{2,1,0:T(8,128)}) custom-call(f32[10,256,128]{2,1,0:T(8,128)S(1)} %get-tuple-element.7.sums_ref, f32[256,256]{1,0:T(8,128)S(1)} %get-tuple-element.8.inverse, f32[2,1024,128]{2,1,0:T(8,128)S(1)} %get-tuple-element.9.panels, f32[10,1024,128]{2,1,0:T(8,128)} %bitcast.4), custom_call_target="tpu_custom_call" | custom-call | tf_op jit(solution)/shard_map/reduce_columns/pallas_call | solution.py:354

commit v4 on v3

--- a/solution.py
+++ b/solution.py
@@ -43,10 +43,6 @@
     rounds, rows_dev, blk = columns.shape
     piece = rows_dev // PIECES
 
-    loads = [pltpu.make_async_copy(c_hbm.at[r], columns.at[r], load_sem.at[r]) for r in range(rounds)]
-    for load in loads:
-        load.start()
-
     barrier = pltpu.get_barrier_semaphore()
     for far in range(1, n):
         pl.semaphore_signal(barrier, inc=1, device_id=(lax.rem(row + far, n), col), device_id_type=MESH)
@@ -81,11 +77,15 @@
                for at in range(PIECES)]
         for copy in own:
             copy.start()
-        for copy in own:
-            copy.wait()
-
+        for at in range(PIECES):
+            own[at].wait()
+            if chips > 1:
+                along(at).start()
+            across(at).start()
+
+    loads = [pltpu.make_async_copy(c_hbm.at[r], columns.at[r], load_sem.at[r]) for r in range(rounds)]
     for load in loads:
-        load.wait()
+        load.start()
 
     owners = min(n, blk // 8)
     share = blk // owners
@@ -153,16 +153,62 @@
         work[half(1 - core), :2 * blk] = other[...]
         work[:, 2 * blk:] = jnp.where(across_ == down, 1.0, 0.0).astype(jnp.float32)
 
+    wide = 2 * blk
+    bits = n.bit_length() - 1
+    plain = list(range(bits))
+    swapped = [1, 0] + plain[2:] if bits > 1 else plain
+    chains = [(first, swapped if first == 2 else plain) for first in range(0, rounds, 2)]
+    items = eliminate(work, inverse)
+
+    def side(bit):
+        return (row // 2 ** bit) % 2
+
+    def partner(bit):
+        return row + (1 - 2 * side(bit)) * 2 ** bit
+
+    def start_of(order, phases):
+        at = 0
+        for t in range(phases):
+            at = at + side(order[t]) * (wide >> (t + 1))
+        return at
+
+    def span_of(at, size):
+        return pl.ds(pl.multiple_of(at, 8), size)
+
+    def halve(which, t):
+        first, order = chains[which]
+        over, size = pl.ds(first, 2), wide >> (t + 1)
+        sent = start_of(order, t) + (1 - side(order[t])) * size
+        return remote(cross.at[over, span_of(sent, size)], slots.at[over, pl.ds(wide - 2 * size, size)],
+                      rs_send.at[which, t], rs_recv.at[which, t], partner(order[t]), col)
+
+    def double(which, t):
+        first, order = chains[which]
+        size = wide >> (t + 1)
+        held = total.at[pl.ds(first, 2), span_of(start_of(order, t + 1), size)]
+        return remote(held, held, ag_send.at[which, t], ag_recv.at[which, t], partner(order[t]), col)
+
+    def add(which, t):
+        first, order = chains[which]
+        over, size = pl.ds(first, 2), wide >> (t + 1)
+        kept_rows = span_of(start_of(order, t + 1), size)
+        into = total if t == bits - 1 else cross
+        into[over, kept_rows, :] = cross[over, kept_rows, :] + slots[over, pl.ds(wide - 2 * size, size), :]
+
     for at in range(PIECES):
         @pl.when(chip > 0)
         def _():
             along(at).wait_recv()
 
-        @pl.when(chip < chips - 1)
-        def _():
-            along(at).start()
-
-        across(at).start()
+            @pl.when(chip < chips - 1)
+            def _():
+                along(at).start()
+
+            across(at).start()
+
+        if at == 0:
+            for load in loads:
+                load.wait()
         from_sibling(at).wait_recv()
         rows = pl.ds(at * piece, piece)
         both = jnp.concatenate([panels[0, rows, :], panels[1, rows, :]], axis=1)
@@ -180,58 +226,18 @@
             else:
                 cross[r] = term[:, :blk]
                 cross[r + 1] = term[:, blk:]
-
-    wide = 2 * blk
-    bits = n.bit_length() - 1
-    plain = list(range(bits))
-    swapped = [1, 0] + plain[2:] if bits > 1 else plain
-    chains = [(first, plain if first % 4 == 0 else swapped) for first in range(0, rounds, 2)]
-    items = eliminate(work, inverse)
-
-    def side(bit):
-        return (row // 2 ** bit) % 2
-
-    def partner(bit):
-        return row + (1 - 2 * side(bit)) * 2 ** bit
-
-    def start_of(order, phases):
-        at = 0
-        for t in range(phases):
-            at = at + side(order[t]) * (wide >> (t + 1))
-        return at
-
-    def span_of(at, size):
-        return pl.ds(pl.multiple_of(at, 8), size)
-
-    def halve(which, t):
-        first, order = chains[which]
-        over, size = pl.ds(first, 2), wide >> (t + 1)
-        sent = start_of(order, t) + (1 - side(order[t])) * size
-        return remote(cross.at[over, span_of(sent, size)], slots.at[over, pl.ds(wide - 2 * size, size)],
-                      rs_send.at[which, t], rs_recv.at[which, t], partner(order[t]), col)
-
-    def double(which, t):
-        first, order = chains[which]
-        size = wide >> (t + 1)
-        held = total.at[pl.ds(first, 2), span_of(start_of(order, t + 1), size)]
-        return remote(held, held, ag_send.at[which, t], ag_recv.at[which, t], partner(order[t]), col)
-
-    def add(which, t):
-        first, order = chains[which]
-        over, size = pl.ds(first, 2), wide >> (t + 1)
-        kept_rows = span_of(start_of(order, t + 1), size)
-        into = total if t == bits - 1 else cross
-        into[over, kept_rows, :] = cross[over, kept_rows, :] + slots[over, pl.ds(wide - 2 * size, size), :]
+            if at == PIECES - 1:
+                halve(r // 2, 0).start()
 
     early = [gather_gram, swap_gram, place_gram]
-    for which in range(len(chains)):
-        halve(which, 0).start()
     for t in range(2 * bits):
         for which in range(len(chains)):
             if early:
                 early.pop(0)()
             else:
                 next(items, None)
+                if which == 0:
+                    next(items, None)
             if t < bits:
                 halve(which, t).wait_recv()
                 add(which, t)
@@ -327,19 +333,21 @@
         yield
 
 
-def reduce_kernel(sums_ref, inverse, panels, c_ref, reduced, top_rows, high, low):
+def reduce_kernel(sums_ref, inverse, panels, c_ref, reduced, top_rows, high, low, forward, backward):
     blk = c_ref.shape[2]
     step = pl.program_id(0)
 
     @pl.when(step == 0)
     def _():
+        forward[0], forward[1] = split(inverse[...])
+        backward[0], backward[1] = split(inverse[...].T)
         high[...], low[...] = split(jnp.concatenate([panels[0], panels[1]], axis=1))
 
     cross = jnp.concatenate([sums_ref[2 * step], sums_ref[2 * step + 1]], axis=1)
-    weights = product(inverse[...], cross, (1, 0))
+    weights = split_product((forward[0], forward[1]), split(cross))
     top_rows[0] = weights[:, :blk]
     top_rows[1] = weights[:, blk:]
-    coefficients = product(inverse[...], weights, (0, 0))
+    coefficients = split_product((backward[0], backward[1]), split(weights))
     span = split_product((high[...], low[...]), split(coefficients))
     reduced[0] = c_ref[0] - span[:, :blk]
     reduced[1] = c_ref[1] - span[:, blk:]
@@ -357,7 +365,7 @@
         out_shape=(shape(block.shape, jnp.float32), shape((rounds, wide, blk), jnp.float32)),
         in_specs=[whole(total), whole(inverse), whole(panels), pair],
         out_specs=(pair, pl.BlockSpec((2, wide, blk), lambda i: (i, 0, 0))),
-        scratch_shapes=[pltpu.VMEM((rows_dev, wide), jnp.bfloat16)] * 2,
+        scratch_shapes=[pltpu.VMEM((rows_dev, wide), jnp.bfloat16)] * 2 + [pltpu.VMEM((2, wide, wide), jnp.bfloat16)] * 2,
         compiler_params=pltpu.CompilerParams(vmem_limit_bytes=48 * 2**20),
         name="reduce_columns",
     )(total, inverse, panels, block)

time: 78.9 us -> 81 us (1.027)
  Pallas kernels: 78 us -> 79.9 us
    pallas_call x1, Pallas kernels: 67.3 us -> 70.2 us  [sums(): pl.pallas_call(functools.partial(sums_kernel, n, chips), out_shape=(shape...]
    pallas_call x1, Pallas kernels: 10.6 us -> 9.72 us  [reduce(): pl.pallas_call(reduce_kernel, grid=(rounds // 2,), out_shape=(shape(block...]
where the time goes in v4:
time: 81 us; the launch traced here: 80.6 us
  Pallas kernels  79.9 us (99%)
    pallas_call x1, Pallas kernels, sums(): pl.pallas_call(functools.partial(sums_kernel, n, chips), out_shape=(shape...  70.2 us
    pallas_call x1, Pallas kernels, reduce(): pl.pallas_call(reduce_kernel, grid=(rounds // 2,), out_shape=(shape(block...  9.72 us

profile of v4, /device:TPU:2, one launch (start us, length us, event | category | flops | bytes accessed | tf_op | source)
XLA Modules:
  0.0 80.6 jit_solution(9895284206004200604)
XLA Ops:
  0.6 70.2 %panel_sums.1 = (f32[2,1024,128]{2,1,0:T(8,128)S(1)}, f32[10,256,128]{2,1,0:T(8,128)S(1)}, f32[256,256]{1,0:T(8,128)S(1)}) custom-call(f32[10,1024,128]{2,1,0:T(8,128)} %bitcast.3), custom_call_target="tpu_custom_call" | custom-call | tf_op jit(solution)/shard_map/panel_sums/pallas_call | solution.py:272
  70.9 9.7 %reduce_columns.1 = (f32[10,1024,128]{2,1,0:T(8,128)}, f32[10,256,128]{2,1,0:T(8,128)}) custom-call(f32[10,256,128]{2,1,0:T(8,128)S(1)} %get-tuple-element.7.sums_ref, f32[256,256]{1,0:T(8,128)S(1)} %get-tuple-element.8.inverse, f32[2,1024,128]{2,1,0:T(8,128)S(1)} %get-tuple-element.9.panels, f32[10,1024,128]{2,1,0:T(8,128)} %bitcast.4), custom_call_target="tpu_custom_call" | custom-call | tf_op jit(solution)/shard_map/reduce_columns/pallas_call | solution.py:362

commit v5 on v4

--- a/solution.py
+++ b/solution.py
@@ -25,8 +25,9 @@
 
 
 def split_product(left, right):
-    dot = functools.partial(jnp.dot, preferred_element_type=jnp.float32)
-    return dot(left[0], right[0]) + (dot(left[0], right[1]) + dot(left[1], right[0]))
+    deep_left = jnp.concatenate([left[0], left[0], left[1]], axis=1)
+    deep_right = jnp.concatenate([right[1], right[0], right[0]], axis=0)
+    return jnp.dot(deep_left, deep_right, preferred_element_type=jnp.float32)
 
 
 def remote(src, dst, send, recv, row, col):
@@ -157,7 +158,7 @@
     bits = n.bit_length() - 1
     plain = list(range(bits))
     swapped = [1, 0] + plain[2:] if bits > 1 else plain
-    chains = [(first, swapped if first == 2 else plain) for first in range(0, rounds, 2)]
+    chains = [(first, plain if first % 4 == 0 else swapped) for first in range(0, rounds, 2)]
     items = eliminate(work, inverse)
 
     def side(bit):
@@ -236,8 +237,6 @@
                 early.pop(0)()
             else:
                 next(items, None)
-                if which == 0:
-                    next(items, None)
             if t < bits:
                 halve(which, t).wait_recv()
                 add(which, t)

time: 81 us -> 78.4 us (0.968)
  Pallas kernels: 79.9 us -> 77.4 us
    pallas_call x1, Pallas kernels: 70.2 us -> 67.7 us  [sums(): pl.pallas_call(functools.partial(sums_kernel, n, chips), out_shape=(shape...]
where the time goes in v5:
time: 78.4 us; the launch traced here: 78.1 us
  Pallas kernels  77.4 us (99%)
    pallas_call x1, Pallas kernels, sums(): pl.pallas_call(functools.partial(sums_kernel, n, chips), out_shape=(shape...  67.7 us
    pallas_call x1, Pallas kernels, reduce(): pl.pallas_call(reduce_kernel, grid=(rounds // 2,), out_shape=(shape(block...  9.73 us

profile of v5, /device:TPU:2, one launch (start us, length us, event | category | flops | bytes accessed | tf_op | source)
XLA Modules:
  0.0 78.1 jit_solution(10157808824560332966)
XLA Ops:
  0.6 67.7 %panel_sums.1 = (f32[2,1024,128]{2,1,0:T(8,128)S(1)}, f32[10,256,128]{2,1,0:T(8,128)S(1)}, f32[256,256]{1,0:T(8,128)S(1)}) custom-call(f32[10,1024,128]{2,1,0:T(8,128)} %bitcast.3), custom_call_target="tpu_custom_call" | custom-call | tf_op jit(solution)/shard_map/panel_sums/pallas_call | solution.py:271
  68.4 9.7 %reduce_columns.1 = (f32[10,1024,128]{2,1,0:T(8,128)}, f32[10,256,128]{2,1,0:T(8,128)}) custom-call(f32[10,256,128]{2,1,0:T(8,128)S(1)} %get-tuple-element.7.sums_ref, f32[256,256]{1,0:T(8,128)S(1)} %get-tuple-element.8.inverse, f32[2,1024,128]{2,1,0:T(8,128)S(1)} %get-tuple-element.9.panels, f32[10,1024,128]{2,1,0:T(8,128)} %bitcast.4), custom_call_target="tpu_custom_call" | custom-call | tf_op jit(solution)/shard_map/reduce_columns/pallas_call | solution.py:361

commit v6 on v5

--- a/solution.py
+++ b/solution.py
@@ -158,7 +158,7 @@
     bits = n.bit_length() - 1
     plain = list(range(bits))
     swapped = [1, 0] + plain[2:] if bits > 1 else plain
-    chains = [(first, plain if first % 4 == 0 else swapped) for first in range(0, rounds, 2)]
+    chains = [(first, plain if first % 4 == 2 else swapped) for first in range(0, rounds, 2)]
     items = eliminate(work, inverse)
 
     def side(bit):

time: 78.4 us -> 79.3 us (1.011)
  no operation moved by 1% of the time
where the time goes in v6:
time: 79.3 us; the launch traced here: 78.7 us
  Pallas kernels  78 us (98%)
    pallas_call x1, Pallas kernels, sums(): pl.pallas_call(functools.partial(sums_kernel, n, chips), out_shape=(shape...  68.3 us
    pallas_call x1, Pallas kernels, reduce(): pl.pallas_call(reduce_kernel, grid=(rounds // 2,), out_shape=(shape(block...  9.73 us

profile of v6, /device:TPU:2, one launch (start us, length us, event | category | flops | bytes accessed | tf_op | source)
XLA Modules:
  0.0 78.7 jit_solution(4965331915947659520)
XLA Ops:
  0.6 68.3 %panel_sums.1 = (f32[2,1024,128]{2,1,0:T(8,128)S(1)}, f32[10,256,128]{2,1,0:T(8,128)S(1)}, f32[256,256]{1,0:T(8,128)S(1)}) custom-call(f32[10,1024,128]{2,1,0:T(8,128)} %bitcast.3), custom_call_target="tpu_custom_call" | custom-call | tf_op jit(solution)/shard_map/panel_sums/pallas_call | solution.py:271
  68.9 9.7 %reduce_columns.1 = (f32[10,1024,128]{2,1,0:T(8,128)}, f32[10,256,128]{2,1,0:T(8,128)}) custom-call(f32[10,256,128]{2,1,0:T(8,128)S(1)} %get-tuple-element.7.sums_ref, f32[256,256]{1,0:T(8,128)S(1)} %get-tuple-element.8.inverse, f32[2,1024,128]{2,1,0:T(8,128)S(1)} %get-tuple-element.9.panels, f32[10,1024,128]{2,1,0:T(8,128)} %bitcast.4), custom_call_target="tpu_custom_call" | custom-call | tf_op jit(solution)/shard_map/reduce_columns/pallas_call | solution.py:361
